TPU v7x, 32 devices: a whole 2x2x4 slice. The times are simulated.
32 devices in a mesh: dom: 16 (over z, y, core), feat: 2 (over x).
Axes of the slice: x: 2, y: 2, z: 4, core: 2. Of those that a mesh axis runs over, the one named last changes fastest.
Arguments:
- node_features: bfloat16 [16384, 128], P('dom'), may hold values from -6 to 6
- weight: bfloat16 [128, 256], P(None, 'feat'), may hold values from -0.5 to 0.5
- bias: float32 [256], P('feat'), may hold values from -3 to 3
- tile_values: bfloat16 [1536, 128, 128], P('dom')
- tile_src: int32 [1536], P('dom'), may hold values from 0 to 7
- tile_dst: int32 [1536], P('dom'), may hold values from 0 to 31, as said below
- tile_counts: int32 [16], P('dom'), may hold values from 4 to 96
- out_grad: bfloat16 [16384, 256], P('dom', 'feat'), may hold values from -6 to 6
Outputs:
- output: bfloat16 [16384, 256], P('dom', 'feat')
- weight_grad: float32 [128, 256], P(None, 'feat')
- bias_grad: float32 [256], P('feat')
- input_grad: bfloat16 [16384, 128], P('dom', 'feat')
Inputs may be any that keep to these rules, and one draw needn't show every extreme that they name: The partition offset tile_dst[k] // 8 of slot k of a partition equals k mod 4.
All inputs are finite; a program needn't handle non-finite values.
Results may differ from a plain program's by a relative error of at most 0.0075.
Values may be sent and summed in bfloat16 or wider, within the bound.
No kernel may reach another device: no remote copies, remote signals or barrier semaphores. Data moves between devices by JAX's collectives and lax.ppermute only.
A program may use at most 64 MiB of HBM per device.

v0:
```python
import functools

import jax
import jax.numpy as jnp
from jax import lax
from jax.experimental import pallas as pl
from jax.experimental.pallas import tpu as pltpu
from jax.sharding import PartitionSpec as P

BLOCK = 128
REACH = 4
F32 = jnp.float32
BF16 = jnp.bfloat16
VMEM = pl.BlockSpec(memory_space=pltpu.VMEM)
SMEM = pl.BlockSpec(memory_space=pltpu.SMEM)
HBM = pl.BlockSpec(memory_space=pltpu.HBM)


def call(kernel, out_shape, in_specs, out_specs, scratch=(), flops=0):
    return pl.pallas_call(
        kernel,
        out_shape=out_shape,
        in_specs=in_specs,
        out_specs=out_specs,
        scratch_shapes=list(scratch),
        compiler_params=pltpu.CompilerParams(vmem_limit_bytes=24 * 1024 * 1024),
        cost_estimate=pl.CostEstimate(flops=flops, bytes_accessed=2**20, transcendentals=0),
    )


def groups_at_once(groups):
    return next(m for m in (4, 3, 2, 1) if groups % m == 0)


def in_hbm(a):
    return pltpu.with_memory_space_constraint(a, pltpu.HBM)


def own_core():
    return lax.rem(lax.axis_index("dom"), 2)


def slot_loop(count, groups, offsets, body, arrive=None):
    m = groups_at_once(groups)

    def chunk(i, carry):
        if arrive is not None:
            arrive(i)

        @pl.when(i * (m * REACH) < count)
        def _():
            for u in range(m):
                for o in offsets:
                    j = i * m + u
                    body(j, o, j * REACH + o < count)

        return carry

    lax.fori_loop(0, groups // m, chunk, 0)


def push(xt, tiles_ref, src_ref, dst_ref, acc, j, o, live):
    blocks = xt.shape[0]
    k = j * REACH + o
    d = jnp.where(live, dst_ref[k] - o * blocks, blocks)
    acc[d] += lax.dot_general(
        xt[src_ref[k]], tiles_ref[j, o], (((1,), (1,)), ((), ())), preferred_element_type=F32
    )


def forward_swap_kernel(
    count, src_hbm, dst_hbm, x_hbm, tiles_hbm, tiles, xt, swap, src, dst, x, acc, small, large
):
    blocks, width, _ = xt.shape
    groups = tiles.shape[0]
    m = groups_at_once(groups)
    copies = [
        pltpu.make_async_copy(a, b, small.at[i])
        for i, (a, b) in enumerate(((x_hbm, x), (src_hbm, src), (dst_hbm, dst)))
    ]

    def chunk(i):
        part = pl.ds(i * m, m)
        return pltpu.make_async_copy(tiles_hbm.at[part], tiles.at[part], large.at[i])

    for c in copies:
        c.start()
    for i in range(groups // m):
        chunk(i).start()
    acc[...] = jnp.zeros_like(acc)
    row = lax.broadcasted_iota(jnp.int32, (width, x.shape[1]), 0)
    column = lax.broadcasted_iota(jnp.int32, (width, x.shape[1]), 1)
    pick = (column == row + lax.axis_index("feat") * width).astype(BF16)
    for c in copies:
        c.wait()
    for b in range(blocks):
        xt[b] = lax.dot_general(
            pick, x[b * BLOCK : (b + 1) * BLOCK, :], (((1,), (1,)), ((), ())), preferred_element_type=F32
        ).astype(BF16)
    o = 3 - 2 * own_core()
    slot_loop(
        count[0], groups, (o,), functools.partial(push, xt, tiles, src, dst, acc), lambda i: chunk(i).wait()
    )
    swap[...] = acc[:blocks].astype(BF16)


def forward_send_kernel(count, src, dst, xt, tiles, acc2, direct, acc):
    acc2[...] = jnp.zeros_like(acc2)
    acc[...] = jnp.zeros_like(acc)
    far = 1 + 2 * own_core()

    def body(j, o, live):
        push(xt, tiles, src, dst, acc2 if isinstance(o, int) else acc, j, o, live)

    slot_loop(count[0], tiles.shape[0], (2, far), body)
    direct[...] = acc[: direct.shape[0]].astype(BF16)


def forward_own_kernel(count, src, dst, xt, tiles, acc):
    acc[...] = jnp.zeros_like(acc)
    slot_loop(count[0], tiles.shape[0], (0,), functools.partial(push, xt, tiles, src, dst, acc))


def sum_kernel(n, first, *refs):
    for out in refs[n:]:
        blocks = out.shape[0]
        total = None
        for r in refs[:n]:
            part = r[...] if r.shape[0] == blocks else r[first : first + blocks]
            total = part.astype(F32) if total is None else total + part.astype(F32)
        out[...] = total.astype(out.dtype)
        first += blocks


def join_kernel(parts, *refs):
    out = refs[-1]
    halves = [refs[i : i + parts] for i in range(0, len(refs) - 1, parts)]
    first = 0
    for half in halves:
        blocks = half[0].shape[0]
        total = half[0][...].astype(F32)
        for r in half[1:]:
            total = total + r[...].astype(F32)
        out[first : first + blocks] = total.astype(out.dtype)
        first += blocks


def middle_kernel(parts, first, bias_ref, w_ref, og_ref, *refs):
    h_refs, (act, ht, grads), g_refs = refs[:parts], refs[parts : parts + 3], refs[parts + 3 :]
    blocks, width, _ = h_refs[0].shape
    f_in = w_ref.shape[0]
    me = lax.axis_index("feat")
    for q in range(parts):
        row = pl.multiple_of(lax.rem(me + q, parts) * width, width)
        for b in range(blocks):
            ht[pl.ds(row, width), b * BLOCK : (b + 1) * BLOCK] = h_refs[q][b]
    ht[f_in:, :] = jnp.ones((ht.shape[0] - f_in, ht.shape[1]), BF16)
    for b in range(blocks):
        rows = slice(b * BLOCK, (b + 1) * BLOCK)
        pre = lax.dot_general(
            ht[:f_in, rows], w_ref[...], (((0,), (0,)), ((), ())), preferred_element_type=F32
        ) + bias_ref[...]
        s = jax.nn.sigmoid(pre)
        act[rows, :] = (pre * s).astype(BF16)
        og = og_ref[(first + b) * BLOCK : (first + b + 1) * BLOCK, :].astype(F32)
        grad = (og * s * (1.0 + pre * (1.0 - s))).astype(BF16)
        grads[rows, :] = grad
        for q in range(parts):
            row = pl.multiple_of(lax.rem(me + q, parts) * width, width)
            g_refs[q][b] = lax.dot_general(
                w_ref[pl.ds(row, width), :], grad, (((1,), (1,)), ((), ())), preferred_element_type=F32
            ).astype(g_refs[q].dtype)


def weight_grad_kernel(n, *refs):
    hts, grads, acts, (out, wg, sems) = refs[:n], refs[n : 2 * n], refs[2 * n : 3 * n], refs[3 * n :]
    copies, first = [], 0
    for i, act in enumerate(acts):
        rows = act.shape[0]
        copies.append(pltpu.make_async_copy(act, out.at[pl.ds(first, rows)], sems.at[i]))
        copies[-1].start()
        first += rows
    full = sum(jnp.dot(h[...], g[...], preferred_element_type=F32) for h, g in zip(hts, grads))
    wg[...] = full[: wg.shape[0]].astype(wg.dtype)
    for c in copies:
        c.wait()


def pull(g, tiles, src, dst, acc, j, o, live):
    blocks = g.shape[0]
    k = j * REACH + o
    s = jnp.where(live, src[k], blocks)
    acc[s] += jnp.dot(g[dst[k] - o * blocks], tiles[j, o], preferred_element_type=F32)


def backward_own_kernel(count, src, dst, tiles, g0, acc):
    acc[...] = jnp.zeros_like(acc)
    slot_loop(count[0], tiles.shape[0], (0,), functools.partial(pull, g0, tiles, src, dst, acc))


def backward_near_kernel(count, src, dst, tiles, g2, gd, acc2, accd):
    acc2[...] = jnp.zeros_like(acc2)
    accd[...] = jnp.zeros_like(accd)
    far = 1 + 2 * own_core()

    def body(j, o, live):
        if isinstance(o, int):
            pull(g2, tiles, src, dst, acc2, j, o, live)
        else:
            pull(gd, tiles, src, dst, accd, j, o, live)

    slot_loop(count[0], tiles.shape[0], (2, far), body)


def backward_last_kernel(count, src, dst, tiles, g, acc0, acc2, accd, *refs):
    parts, (out, wg, bias, acc) = refs[:-4], refs[-4:]
    blocks = g.shape[0]
    acc[...] = jnp.zeros_like(acc)
    far = 3 - 2 * own_core()
    slot_loop(count[0], tiles.shape[0], (far,), functools.partial(pull, g, tiles, src, dst, acc))
    for b in range(blocks):
        total = acc[b] + acc0[b] + acc2[b] + accd[b]
        out[:, b * BLOCK : (b + 1) * BLOCK] = total.astype(BF16)
    whole = paired_sum([r[...] for r in parts])
    f_in = wg.shape[0]
    wg[...] = whole[:f_in]
    bias[...] = whole[f_in : f_in + 1]


def paired_sum(parts):
    parts = [p.astype(F32) for p in parts]
    while len(parts) > 1:
        parts = [parts[i] + parts[i + 1] for i in range(0, len(parts), 2)]
    return parts[0]


def paired_sum_kernel(*refs):
    refs[-1][...] = paired_sum([r[...] for r in refs[:-1]]).astype(refs[-1].dtype)


def moved(block, axis, target):
    n = lax.axis_size(axis)
    return lax.ppermute(block, axis, [(i, target(i) % n) for i in range(n)])


def radices(n):
    out = []
    while n > 1:
        r = 4 if n % 4 == 0 else 2
        out.append(r)
        n //= r
    return out


def exchanged(part, axis, stride, r):
    return [part] + [moved(part, axis, lambda i, s=s: i ^ (s * stride)) for s in range(1, r)]


def shards(node_features, weight, bias, tile_values, tile_src, tile_dst, tile_counts, out_grad):
    nodes, f_in = node_features.shape
    hid = weight.shape[1]
    blocks = nodes // BLOCK
    parts = lax.axis_size("feat")
    width = f_in // parts
    capacity = tile_values.shape[0]
    groups = capacity // REACH
    piece = jax.ShapeDtypeStruct((blocks, width, BLOCK), BF16)
    totals = jax.ShapeDtypeStruct((blocks + 1, width, BLOCK), F32)
    acc = pltpu.VMEM(totals.shape, F32)
    tiles = jax.ShapeDtypeStruct((groups, REACH, BLOCK, BLOCK), BF16)
    slots = jax.ShapeDtypeStruct((capacity,), jnp.int32)
    rows = jax.ShapeDtypeStruct((nodes, hid), BF16)
    gradient = jax.ShapeDtypeStruct((f_in + 16, hid), BF16)
    m = groups_at_once(groups)
    flops = 2 * capacity * BLOCK * BLOCK * width // REACH

    def swapped(i):
        return i ^ 1

    tiles, xt, swap, src, dst = call(
        forward_swap_kernel,
        [tiles, piece, piece, slots, slots],
        [SMEM] + [HBM] * 4,
        [VMEM] * 3 + [SMEM] * 2,
        [
            pltpu.VMEM(node_features.shape, BF16),
            acc,
            pltpu.SemaphoreType.DMA((3,)),
            pltpu.SemaphoreType.DMA((groups // m,)),
        ],
        flops,
    )(tile_counts, *(in_hbm(a) for a in (tile_src, tile_dst, node_features, tile_values.reshape(tiles.shape))))
    index = (tile_counts, src, dst)
    swap = moved(swap, "dom", swapped)
    acc2, direct = call(
        forward_send_kernel, [totals, piece], [SMEM] * 3 + [VMEM] * 2, [VMEM] * 2, [acc], 2 * flops
    )(*index, xt, tiles)
    cut = 2 if blocks % 2 == 0 else 1
    starts = range(0, blocks, blocks // cut)
    half = jax.ShapeDtypeStruct((blocks // cut, width, BLOCK), BF16)
    half_wide = jax.ShapeDtypeStruct(half.shape, F32)
    half_rows = jax.ShapeDtypeStruct((nodes // cut, hid), BF16)
    half_columns = jax.ShapeDtypeStruct((f_in + 16, nodes // cut), BF16)
    chip = call(functools.partial(sum_kernel, 2, 0), [half] * cut, [VMEM] * 2, [VMEM] * cut)(acc2, swap)
    chip = [moved(c, "dom", lambda i: i + 2) for c in chip]
    direct = moved(direct, "dom", lambda i: i + 1 + 2 * (i % 2))
    (acc0,) = call(forward_own_kernel, [totals], [SMEM] * 3 + [VMEM] * 2, [VMEM], (), flops)(*index, xt, tiles)
    h_lists = []
    for first, c in zip(starts, chip):
        (h,) = call(functools.partial(sum_kernel, 3, first), [half], [VMEM] * 3, [VMEM])(acc0, direct, c)
        h_lists.append([h] + [moved(h, "feat", lambda i, q=q: i - q) for q in range(1, parts)])
    acts, hts, grads, g_list = [], [], [], []
    for first, hs in zip(starts, h_lists):
        act, ht, grad, g_own, *g_others = call(
            functools.partial(middle_kernel, parts, first),
            [half_rows, half_columns, half_rows, half_wide] + [half] * (parts - 1),
            [VMEM] * (3 + parts),
            [VMEM] * (3 + parts),
            (),
            4 * nodes * f_in * hid // cut,
        )(bias.reshape(1, hid), weight, out_grad, *hs)
        acts.append(act)
        hts.append(ht)
        grads.append(grad)
        g_list += [g_own] + [moved(g, "feat", lambda i, q=q + 1: i + q) for q, g in enumerate(g_others)]
    output, wg = call(
        functools.partial(weight_grad_kernel, cut),
        [rows, gradient],
        [VMEM] * (3 * cut),
        [HBM, VMEM],
        [pltpu.SemaphoreType.DMA((cut,))],
        2 * nodes * f_in * hid,
    )(*hts, *grads, *acts)
    r, *more = radices(lax.axis_size("dom"))
    wgs = exchanged(wg, "dom", 1, r)
    g_list[0], wgs[1] = lax.optimization_barrier((g_list[0], wgs[1]))
    (g,) = call(functools.partial(join_kernel, parts), [piece], [VMEM] * len(g_list), [VMEM])(*g_list)
    g_chip = moved(g, "dom", lambda i: i - 2)
    g_direct = moved(g, "dom", lambda i: i - 3 + 2 * (i % 2))
    (back0,) = call(backward_own_kernel, [totals], [SMEM] * 3 + [VMEM] * 2, [VMEM], (), flops)(*index, tiles, g)
    stride = r
    for r in more:
        back0, *wgs = lax.optimization_barrier((back0, *wgs))
        (wg,) = call(paired_sum_kernel, [gradient], [VMEM] * len(wgs), [VMEM])(*wgs)
        wgs = exchanged(wg, "dom", stride, r)
        stride *= r
    g_chip, g_direct, *wgs = lax.optimization_barrier((g_chip, g_direct, *wgs))
    g_swap = moved(g_chip, "dom", swapped)
    back2, backd = call(
        backward_near_kernel, [totals, totals], [SMEM] * 3 + [VMEM] * 3, [VMEM] * 2, (), 2 * flops
    )(*index, tiles, g_chip, g_direct)
    input_grad, weight_grad, bias_grad = call(
        backward_last_kernel,
        [
            jax.ShapeDtypeStruct((width, nodes), BF16),
            jax.ShapeDtypeStruct((f_in, hid), F32),
            jax.ShapeDtypeStruct((1, hid), F32),
        ],
        [SMEM] * 3 + [VMEM] * (5 + len(wgs)),
        [VMEM] * 3,
        [acc],
        flops,
    )(*index, tiles, g_swap, back0, back2, backd, *wgs)
    return output, weight_grad, bias_grad.reshape(hid), input_grad.T


def solution(mesh):
    return jax.shard_map(
        shards,
        mesh=mesh,
        in_specs=(
            P("dom", None),
            P(None, "feat"),
            P("feat"),
            P("dom", None, None),
            P("dom"),
            P("dom"),
            P("dom"),
            P("dom", "feat"),
        ),
        out_specs=(P("dom", "feat"), P(None, "feat"), P("feat"), P("dom", "feat")),
        check_vma=False,
    )
```

profile of v0, /device:TPU:0, one launch (start us, length us, event | category | flops | bytes accessed | tf_op | source)
XLA Modules:
  0.0 46.3 jit_solution(7369047739635074724)
XLA Ops:
  1.3 2.9 %shard_map.111 = (bf16[24,4,128,128]{3,2,1,0:T(8,128)(2,1)S(1)}, bf16[8,64,128]{2,1,0:T(8,128)(2,1)S(1)}, bf16[8,64,128]{2,1,0:T(8,128)(2,1)S(1)}, s32[96]{0:T(128)S(1)}, s32[96]{0:T(128)S(1)}) custom-call(s32[1]{0:T(128)S(6)} %copy.12.count, s32[96]{0:T(128)} %src_hbm.1, s32[96]{0:T(128)} %dst_hbm.1, bf16[1024,128]{1,0:T(8,128)(2,1)} %x_hbm.1, ...), custom_call_target="tpu_custom_call" | custom-call | flops 50331648 | bytes 1048576 | tf_op jit(solution)/shard_map/pallas_call | solution.py:280
  4.9 1.2 %shard_map.113 = (f32[9,64,128]{2,1,0:T(8,128)S(1)}, bf16[8,64,128]{2,1,0:T(8,128)(2,1)S(1)}) custom-call(s32[1]{0:T(128)S(6)} %copy.12.count, s32[96]{0:T(128)S(1)} %get-tuple-element.43.src, s32[96]{0:T(128)S(1)} %get-tuple-element.44.dst, bf16[8,64,128]{2,1,0:T(8,128)(2,1)S(1)} %get-tuple-element.45.xt, bf16[24,4,128,128]{3,2,1,0:T(8,128)(2,1)S(1)} %get-tuple-element.46.tiles), custom_call_target="tpu_custom_call" | custom-call | flops 100663296 | bytes 1048576 | tf_op jit(solution)/shard_map/pallas_call | solution.py:295
  6.5 3.1 %collective-permute-start.4 = (bf16[4,64,128]{2,1,0:T(8,128)(2,1)S(1)}, bf16[4,64,128]{2,1,0:T(8,128)(2,1)S(1)}, u32[]{:S(2)}, u32[]{:S(2)}) collective-permute-start(bf16[4,64,128]{2,1,0:T(8,128)(2,1)S(1)} %get-tuple-element.52), channel_id=1, source_target_pairs={{0,4},{2,6},{4,8},{6,10},{8,12},{10,14},{12,16},{14,18},{16,20},{1... | collective-permute-start | bytes 196616 | tf_op jit(solution)/shard_map/ppermute | solution.py:243
  9.5 1.3 %collective-permute-start.2 = (bf16[4,64,128]{2,1,0:T(8,128)(2,1)S(1)}, bf16[4,64,128]{2,1,0:T(8,128)(2,1)S(1)}, u32[]{:S(2)}, u32[]{:S(2)}) collective-permute-start(bf16[4,64,128]{2,1,0:T(8,128)(2,1)S(1)} %get-tuple-element.50), channel_id=1, source_target_pairs={{0,4},{2,6},{4,8},{6,10},{8,12},{10,14},{12,16},{14,18},{16,20},{1... | collective-permute-start | bytes 196616 | tf_op jit(solution)/shard_map/ppermute | solution.py:243
  10.9 1.0 %shard_map.112.refs_0_ = f32[9,64,128]{2,1,0:T(8,128)S(1)} custom-call(s32[1]{0:T(128)S(6)} %copy.12.count, s32[96]{0:T(128)S(1)} %get-tuple-element.43.src, s32[96]{0:T(128)S(1)} %get-tuple-element.44.dst, bf16[8,64,128]{2,1,0:T(8,128)(2,1)S(1)} %get-tuple-element.45.xt, bf16[24,4,128,128]{3,2,1,0:T(8,128)(2,1)S(1)} %get-tuple-element.46.tiles), custom_call_target="tpu_custom_call" | custom-call | flops 50331648 | bytes 1048576 | tf_op jit(solution)/shard_map/pallas_call | solution.py:307
  11.9 1.7 %collective-permute-done.refs_1_ = bf16[8,64,128]{2,1,0:T(8,128)(2,1)S(1)} collective-permute-done((bf16[8,64,128]{2,1,0:T(8,128)(2,1)S(1)}, bf16[8,64,128]{2,1,0:T(8,128)(2,1)S(1)}, u32[]{:S(2)}, u32[]{:S(2)}) %collective-permute-start) | collective-permute-done | bytes 131104 | tf_op jit(solution)/shard_map/ppermute | solution.py:243
  13.6 2.9 %collective-permute-done.4.refs_2_ = bf16[4,64,128]{2,1,0:T(8,128)(2,1)S(1)} collective-permute-done((bf16[4,64,128]{2,1,0:T(8,128)(2,1)S(1)}, bf16[4,64,128]{2,1,0:T(8,128)(2,1)S(1)}, u32[]{:S(2)}, u32[]{:S(2)}) %collective-permute-start.4) | collective-permute-done | bytes 65568 | tf_op jit(solution)/shard_map/ppermute | solution.py:243
  16.5 1.6 %collective-permute-start.5 = (bf16[4,64,128]{2,1,0:T(8,128)(2,1)S(1)}, bf16[4,64,128]{2,1,0:T(8,128)(2,1)S(1)}, u32[]{:S(2)}, u32[]{:S(2)}) collective-permute-start(bf16[4,64,128]{2,1,0:T(8,128)(2,1)S(1)} %shard_map.117.refs_0_), channel_id=1, source_target_pairs={{0,1},{1,0},{2,3},{3,2},{4,5},{5,4},{6,7},{7,6},{8,9},{9,8},{10,11... | collective-permute-start | bytes 196616 | tf_op jit(solution)/shard_map/ppermute | solution.py:243
  18.1 1.1 %collective-permute-start.3 = (bf16[4,64,128]{2,1,0:T(8,128)(2,1)S(1)}, bf16[4,64,128]{2,1,0:T(8,128)(2,1)S(1)}, u32[]{:S(2)}, u32[]{:S(2)}) collective-permute-start(bf16[4,64,128]{2,1,0:T(8,128)(2,1)S(1)} %shard_map.115.refs_0_), channel_id=1, source_target_pairs={{0,1},{1,0},{2,3},{3,2},{4,5},{5,4},{6,7},{7,6},{8,9},{9,8},{10,11... | collective-permute-start | bytes 196616 | tf_op jit(solution)/shard_map/ppermute | solution.py:243
  19.2 2.1 %collective-permute-done.5.refs_1_ = bf16[4,64,128]{2,1,0:T(8,128)(2,1)S(1)} collective-permute-done((bf16[4,64,128]{2,1,0:T(8,128)(2,1)S(1)}, bf16[4,64,128]{2,1,0:T(8,128)(2,1)S(1)}, u32[]{:S(2)}, u32[]{:S(2)}) %collective-permute-start.5) | collective-permute-done | bytes 65568 | tf_op jit(solution)/shard_map/ppermute | solution.py:243
  21.3 0.9 %shard_map.118 = (bf16[512,128]{1,0:T(8,128)(2,1)S(1)}, bf16[144,512]{1,0:T(8,128)(2,1)S(1)}, bf16[512,128]{1,0:T(8,128)(2,1)S(1)}, f32[4,64,128]{2,1,0:T(8,128)S(1)}, bf16[4,64,128]{2,1,0:T(8,128)(2,1)S(1)}) custom-call(f32[1,128]{1,0:T(1,128)S(1)} %bitcast.4, bf16[128,128]{1,0:T(8,128)(2,1)S(1)} %copy-done.1, bf16[1024,128]{1,0:T(8,128)(2,1)S(1)} %copy-done, ...), custom_call_target="tpu_custom_call" | custom-call | flops 33554432 | bytes 1048576 | tf_op jit(solution)/shard_map/pallas_call | solution.py:314
  22.2 1.8 %collective-permute-start.8 = (bf16[4,64,128]{2,1,0:T(8,128)(2,1)S(1)}, bf16[4,64,128]{2,1,0:T(8,128)(2,1)S(1)}, u32[]{:S(2)}, u32[]{:S(2)}) collective-permute-start(bf16[4,64,128]{2,1,0:T(8,128)(2,1)S(1)} %get-tuple-element.64), channel_id=1, source_target_pairs={{0,1},{1,0},{2,3},{3,2},{4,5},{5,4},{6,7},{7,6},{8,9},{9,8},{10,11... | collective-permute-start | bytes 196616 | tf_op jit(solution)/shard_map/ppermute | solution.py:243
  24.0 0.9 %shard_map.116 = (bf16[512,128]{1,0:T(8,128)(2,1)S(1)}, bf16[144,512]{1,0:T(8,128)(2,1)S(1)}, bf16[512,128]{1,0:T(8,128)(2,1)S(1)}, f32[4,64,128]{2,1,0:T(8,128)S(1)}, bf16[4,64,128]{2,1,0:T(8,128)(2,1)S(1)}) custom-call(f32[1,128]{1,0:T(1,128)S(1)} %bitcast.5, bf16[128,128]{1,0:T(8,128)(2,1)S(1)} %copy-done.1, bf16[1024,128]{1,0:T(8,128)(2,1)S(1)} %copy-done, ...), custom_call_target="tpu_custom_call" | custom-call | flops 33554432 | bytes 1048576 | tf_op jit(solution)/shard_map/pallas_call | solution.py:314
  26.0 1.2 %collective-permute-done.6.refs_1_ = bf16[144,128]{1,0:T(8,128)(2,1)S(1)} collective-permute-done((bf16[144,128]{1,0:T(8,128)(2,1)S(1)}, bf16[144,128]{1,0:T(8,128)(2,1)S(1)}, u32[]{:S(2)}, u32[]{:S(2)}) %collective-permute-start.6) | collective-permute-done | bytes 36896 | tf_op jit(solution)/shard_map/ppermute | solution.py:243
  27.2 2.0 %collective-permute-done.7.refs_1_ = bf16[4,64,128]{2,1,0:T(8,128)(2,1)S(1)} collective-permute-done((bf16[4,64,128]{2,1,0:T(8,128)(2,1)S(1)}, bf16[4,64,128]{2,1,0:T(8,128)(2,1)S(1)}, u32[]{:S(2)}, u32[]{:S(2)}) %collective-permute-start.7) | collective-permute-done | bytes 65568 | tf_op jit(solution)/shard_map/ppermute | solution.py:243
  29.3 0.9 %collective-permute-start.9 = (bf16[8,64,128]{2,1,0:T(8,128)(2,1)S(1)}, bf16[8,64,128]{2,1,0:T(8,128)(2,1)S(1)}, u32[]{:S(2)}, u32[]{:S(2)}) collective-permute-start(bf16[8,64,128]{2,1,0:T(8,128)(2,1)S(1)} %shard_map.120.g0), channel_id=1, source_target_pairs={{0,28},{2,30},{4,0},{6,2},{8,4},{10,6},{12,8},{14,10},{16,12},{18,... | collective-permute-start | bytes 393224 | tf_op jit(solution)/shard_map/ppermute | solution.py:243
  30.1 1.2 %collective-permute-start.11 = (bf16[144,128]{1,0:T(8,128)(2,1)S(1)}, bf16[144,128]{1,0:T(8,128)(2,1)S(1)}, u32[]{:S(2)}, u32[]{:S(2)}) collective-permute-start(bf16[144,128]{1,0:T(8,128)(2,1)S(1)} %get-tuple-element.66.refs_0_), channel_id=1, source_target_pairs={{0,4},{2,6},{4,0},{6,2},{8,12},{10,14},{12,8},{14,10},{16,20},{18,... | collective-permute-start | bytes 110600 | tf_op jit(solution)/shard_map/ppermute | solution.py:243
  31.7 1.0 %shard_map.121.acc0 = f32[9,64,128]{2,1,0:T(8,128)S(1)} custom-call(s32[1]{0:T(128)S(6)} %copy.12.count, s32[96]{0:T(128)S(1)} %get-tuple-element.43.src, s32[96]{0:T(128)S(1)} %get-tuple-element.44.dst, bf16[24,4,128,128]{3,2,1,0:T(8,128)(2,1)S(1)} %get-tuple-element.46.tiles, bf16[8,64,128]{2,1,0:T(8,128)(2,1)S(1)} %shard_map.120.g0), custom_call_target="tpu_custom_call" | custom-call | flops 50331648 | bytes 1048576 | tf_op jit(solution)/shard_map/pallas_call | solution.py:340
  32.6 3.7 %collective-permute-done.11.refs_2_ = bf16[144,128]{1,0:T(8,128)(2,1)S(1)} collective-permute-done((bf16[144,128]{1,0:T(8,128)(2,1)S(1)}, bf16[144,128]{1,0:T(8,128)(2,1)S(1)}, u32[]{:S(2)}, u32[]{:S(2)}) %collective-permute-start.11) | collective-permute-done | bytes 36896 | tf_op jit(solution)/shard_map/ppermute | solution.py:243
  36.5 1.0 %collective-permute-start.14 = (bf16[144,128]{1,0:T(8,128)(2,1)S(1)}, bf16[144,128]{1,0:T(8,128)(2,1)S(1)}, u32[]{:S(2)}, u32[]{:S(2)}) collective-permute-start(bf16[144,128]{1,0:T(8,128)(2,1)S(1)} %shard_map.122.refs_0_), channel_id=1, source_target_pairs={{0,16},{2,18},{4,20},{6,22},{8,24},{10,26},{12,28},{14,30},{16,0},... | collective-permute-start | bytes 110600 | tf_op jit(solution)/shard_map/ppermute | solution.py:243
  37.4 3.4 %collective-permute-start.15 = (bf16[144,128]{1,0:T(8,128)(2,1)S(1)}, bf16[144,128]{1,0:T(8,128)(2,1)S(1)}, u32[]{:S(2)}, u32[]{:S(2)}) collective-permute-start(bf16[144,128]{1,0:T(8,128)(2,1)S(1)} %shard_map.122.refs_0_), channel_id=1, source_target_pairs={{0,24},{2,26},{4,28},{6,30},{8,16},{10,18},{12,20},{14,22},{16,8},... | collective-permute-start | bytes 110600 | tf_op jit(solution)/shard_map/ppermute | solution.py:243
  41.4 1.8 %collective-permute-done.15.refs_3_ = bf16[144,128]{1,0:T(8,128)(2,1)S(1)} collective-permute-done((bf16[144,128]{1,0:T(8,128)(2,1)S(1)}, bf16[144,128]{1,0:T(8,128)(2,1)S(1)}, u32[]{:S(2)}, u32[]{:S(2)}) %collective-permute-start.15) | collective-permute-done | bytes 36896 | tf_op jit(solution)/shard_map/ppermute | solution.py:243
  43.2 1.0 %shard_map.123 = (f32[9,64,128]{2,1,0:T(8,128)S(1)}, f32[9,64,128]{2,1,0:T(8,128)S(1)}) custom-call(s32[1]{0:T(128)S(6)} %copy.12.count, s32[96]{0:T(128)S(1)} %get-tuple-element.43.src, s32[96]{0:T(128)S(1)} %get-tuple-element.44.dst, bf16[24,4,128,128]{3,2,1,0:T(8,128)(2,1)S(1)} %get-tuple-element.46.tiles, ...), custom_call_target="tpu_custom_call" | custom-call | flops 100663296 | bytes 1048576 | tf_op jit(solution)/shard_map/pallas_call | solution.py:349
  44.6 1.7 %shard_map.124 = (bf16[64,1024]{1,0:T(8,128)(2,1)}, f32[128,128]{1,0:T(8,128)}, f32[1,128]{1,0:T(1,128)}) custom-call(s32[1]{0:T(128)S(6)} %copy.12.count, s32[96]{0:T(128)S(1)} %get-tuple-element.43.src, s32[96]{0:T(128)S(1)} %get-tuple-element.44.dst, bf16[24,4,128,128]{3,2,1,0:T(8,128)(2,1)S(1)} %get-tuple-element.46.tiles, ...), custom_call_target="tpu_custom_call" | custom-call | flops 50331648 | bytes 1048576 | tf_op jit(solution)/shard_map/pallas_call | solution.py:352
  (30 shorter events, 3.7 us)
Async XLA Ops:
  4.1 2.3 %collective-permute-start.1 = (bf16[8,64,128]{2,1,0:T(8,128)(2,1)S(1)}, bf16[8,64,128]{2,1,0:T(8,128)(2,1)S(1)}, u32[]{:S(2)}, u32[]{:S(2)}) collective-permute-start(bf16[8,64,128]{2,1,0:T(8,128)(2,1)S(1)} %get-tuple-element.49), channel_id=1, source_target_pairs={{0,2},{2,0},{4,6},{6,4},{8,10},{10,8},{12,14},{14,12},{16,18},{18,... | collective-permute-start | bytes 393224 | tf_op jit(solution)/shard_map/ppermute | solution.py:243
  6.1 15.2 %copy-start = (bf16[1024,128]{1,0:T(8,128)(2,1)S(1)}, bf16[1024,128]{1,0:T(8,128)(2,1)}, u32[]{:S(2)}) copy-start(bf16[1024,128]{1,0:T(8,128)(2,1)} %og_ref.3) | copy-start | bytes 786436
  6.1 15.2 %copy-start.1 = (bf16[128,128]{1,0:T(8,128)(2,1)S(1)}, bf16[128,128]{1,0:T(8,128)(2,1)}, u32[]{:S(2)}) copy-start(bf16[128,128]{1,0:T(8,128)(2,1)} %w_ref.3) | copy-start | bytes 98308
  6.1 15.2 %copy-start.2 = (f32[128]{0:T(128)S(1)}, f32[128]{0:T(128)}, u32[]{:S(2)}) copy-start(f32[128]{0:T(128)} %param.10) | copy-start | bytes 1540
  6.1 7.5 %collective-permute-start = (bf16[8,64,128]{2,1,0:T(8,128)(2,1)S(1)}, bf16[8,64,128]{2,1,0:T(8,128)(2,1)S(1)}, u32[]{:S(2)}, u32[]{:S(2)}) collective-permute-start(bf16[8,64,128]{2,1,0:T(8,128)(2,1)S(1)} %get-tuple-element.47), channel_id=1, source_target_pairs={{0,2},{2,8},{4,6},{6,12},{8,10},{10,16},{12,14},{14,20},{16,18},{1... | collective-permute-start | bytes 393224 | tf_op jit(solution)/shard_map/ppermute | solution.py:243
  6.5 10.0 %collective-permute-start.4 = (bf16[4,64,128]{2,1,0:T(8,128)(2,1)S(1)}, bf16[4,64,128]{2,1,0:T(8,128)(2,1)S(1)}, u32[]{:S(2)}, u32[]{:S(2)}) collective-permute-start(bf16[4,64,128]{2,1,0:T(8,128)(2,1)S(1)} %get-tuple-element.52), channel_id=1, source_target_pairs={{0,4},{2,6},{4,8},{6,10},{8,12},{10,14},{12,16},{14,18},{16,20},{1... | collective-permute-start | bytes 196616 | tf_op jit(solution)/shard_map/ppermute | solution.py:243
  9.5 8.5 %collective-permute-start.2 = (bf16[4,64,128]{2,1,0:T(8,128)(2,1)S(1)}, bf16[4,64,128]{2,1,0:T(8,128)(2,1)S(1)}, u32[]{:S(2)}, u32[]{:S(2)}) collective-permute-start(bf16[4,64,128]{2,1,0:T(8,128)(2,1)S(1)} %get-tuple-element.50), channel_id=1, source_target_pairs={{0,4},{2,6},{4,8},{6,10},{8,12},{10,14},{12,16},{14,18},{16,20},{1... | collective-permute-start | bytes 196616 | tf_op jit(solution)/shard_map/ppermute | solution.py:243
  16.5 4.8 %collective-permute-start.5 = (bf16[4,64,128]{2,1,0:T(8,128)(2,1)S(1)}, bf16[4,64,128]{2,1,0:T(8,128)(2,1)S(1)}, u32[]{:S(2)}, u32[]{:S(2)}) collective-permute-start(bf16[4,64,128]{2,1,0:T(8,128)(2,1)S(1)} %shard_map.117.refs_0_), channel_id=1, source_target_pairs={{0,1},{1,0},{2,3},{3,2},{4,5},{5,4},{6,7},{7,6},{8,9},{9,8},{10,11... | collective-permute-start | bytes 196616 | tf_op jit(solution)/shard_map/ppermute | solution.py:243
  18.1 5.9 %collective-permute-start.3 = (bf16[4,64,128]{2,1,0:T(8,128)(2,1)S(1)}, bf16[4,64,128]{2,1,0:T(8,128)(2,1)S(1)}, u32[]{:S(2)}, u32[]{:S(2)}) collective-permute-start(bf16[4,64,128]{2,1,0:T(8,128)(2,1)S(1)} %shard_map.115.refs_0_), channel_id=1, source_target_pairs={{0,1},{1,0},{2,3},{3,2},{4,5},{5,4},{6,7},{7,6},{8,9},{9,8},{10,11... | collective-permute-start | bytes 196616 | tf_op jit(solution)/shard_map/ppermute | solution.py:243
  22.2 5.0 %collective-permute-start.8 = (bf16[4,64,128]{2,1,0:T(8,128)(2,1)S(1)}, bf16[4,64,128]{2,1,0:T(8,128)(2,1)S(1)}, u32[]{:S(2)}, u32[]{:S(2)}) collective-permute-start(bf16[4,64,128]{2,1,0:T(8,128)(2,1)S(1)} %get-tuple-element.64), channel_id=1, source_target_pairs={{0,1},{1,0},{2,3},{3,2},{4,5},{5,4},{6,7},{7,6},{8,9},{9,8},{10,11... | collective-permute-start | bytes 196616 | tf_op jit(solution)/shard_map/ppermute | solution.py:243
  24.9 4.3 %collective-permute-start.7 = (bf16[4,64,128]{2,1,0:T(8,128)(2,1)S(1)}, bf16[4,64,128]{2,1,0:T(8,128)(2,1)S(1)}, u32[]{:S(2)}, u32[]{:S(2)}) collective-permute-start(bf16[4,64,128]{2,1,0:T(8,128)(2,1)S(1)} %get-tuple-element.62), channel_id=1, source_target_pairs={{0,1},{1,0},{2,3},{3,2},{4,5},{5,4},{6,7},{7,6},{8,9},{9,8},{10,11... | collective-permute-start | bytes 196616 | tf_op jit(solution)/shard_map/ppermute | solution.py:243
  25.9 1.3 %collective-permute-start.6 = (bf16[144,128]{1,0:T(8,128)(2,1)S(1)}, bf16[144,128]{1,0:T(8,128)(2,1)S(1)}, u32[]{:S(2)}, u32[]{:S(2)}) collective-permute-start(bf16[144,128]{1,0:T(8,128)(2,1)S(1)} %get-tuple-element.66.refs_0_), channel_id=1, source_target_pairs={{0,2},{2,0},{4,6},{6,4},{8,10},{10,8},{12,14},{14,12},{16,18},{18,... | collective-permute-start | bytes 110600 | tf_op jit(solution)/shard_map/ppermute | solution.py:243
  29.2 14.0 %collective-permute-start.10 = (bf16[8,64,128]{2,1,0:T(8,128)(2,1)S(1)}, bf16[8,64,128]{2,1,0:T(8,128)(2,1)S(1)}, u32[]{:S(2)}, u32[]{:S(2)}) collective-permute-start(bf16[8,64,128]{2,1,0:T(8,128)(2,1)S(1)} %shard_map.120.g0), channel_id=1, source_target_pairs={{0,26},{2,0},{4,30},{6,4},{8,2},{10,8},{12,6},{14,12},{16,10},{18,... | collective-permute-start | bytes 393224 | tf_op jit(solution)/shard_map/ppermute | solution.py:243
  29.3 14.0 %collective-permute-start.9 = (bf16[8,64,128]{2,1,0:T(8,128)(2,1)S(1)}, bf16[8,64,128]{2,1,0:T(8,128)(2,1)S(1)}, u32[]{:S(2)}, u32[]{:S(2)}) collective-permute-start(bf16[8,64,128]{2,1,0:T(8,128)(2,1)S(1)} %shard_map.120.g0), channel_id=1, source_target_pairs={{0,28},{2,30},{4,0},{6,2},{8,4},{10,6},{12,8},{14,10},{16,12},{18,... | collective-permute-start | bytes 393224 | tf_op jit(solution)/shard_map/ppermute | solution.py:243
  30.1 6.2 %collective-permute-start.11 = (bf16[144,128]{1,0:T(8,128)(2,1)S(1)}, bf16[144,128]{1,0:T(8,128)(2,1)S(1)}, u32[]{:S(2)}, u32[]{:S(2)}) collective-permute-start(bf16[144,128]{1,0:T(8,128)(2,1)S(1)} %get-tuple-element.66.refs_0_), channel_id=1, source_target_pairs={{0,4},{2,6},{4,0},{6,2},{8,12},{10,14},{12,8},{14,10},{16,20},{18,... | collective-permute-start | bytes 110600 | tf_op jit(solution)/shard_map/ppermute | solution.py:243
  31.3 5.0 %collective-permute-start.12 = (bf16[144,128]{1,0:T(8,128)(2,1)S(1)}, bf16[144,128]{1,0:T(8,128)(2,1)S(1)}, u32[]{:S(2)}, u32[]{:S(2)}) collective-permute-start(bf16[144,128]{1,0:T(8,128)(2,1)S(1)} %get-tuple-element.66.refs_0_), channel_id=1, source_target_pairs={{0,6},{2,4},{4,2},{6,0},{8,14},{10,12},{12,10},{14,8},{16,22},{18,... | collective-permute-start | bytes 110600 | tf_op jit(solution)/shard_map/ppermute | solution.py:243
  36.4 4.5 %collective-permute-start.13 = (bf16[144,128]{1,0:T(8,128)(2,1)S(1)}, bf16[144,128]{1,0:T(8,128)(2,1)S(1)}, u32[]{:S(2)}, u32[]{:S(2)}) collective-permute-start(bf16[144,128]{1,0:T(8,128)(2,1)S(1)} %shard_map.122.refs_0_), channel_id=1, source_target_pairs={{0,8},{2,10},{4,12},{6,14},{8,0},{10,2},{12,4},{14,6},{16,24},{18,... | collective-permute-start | bytes 110600 | tf_op jit(solution)/shard_map/ppermute | solution.py:243
  36.5 5.0 %collective-permute-start.14 = (bf16[144,128]{1,0:T(8,128)(2,1)S(1)}, bf16[144,128]{1,0:T(8,128)(2,1)S(1)}, u32[]{:S(2)}, u32[]{:S(2)}) collective-permute-start(bf16[144,128]{1,0:T(8,128)(2,1)S(1)} %shard_map.122.refs_0_), channel_id=1, source_target_pairs={{0,16},{2,18},{4,20},{6,22},{8,24},{10,26},{12,28},{14,30},{16,0},... | collective-permute-start | bytes 110600 | tf_op jit(solution)/shard_map/ppermute | solution.py:243
  37.4 5.8 %collective-permute-start.15 = (bf16[144,128]{1,0:T(8,128)(2,1)S(1)}, bf16[144,128]{1,0:T(8,128)(2,1)S(1)}, u32[]{:S(2)}, u32[]{:S(2)}) collective-permute-start(bf16[144,128]{1,0:T(8,128)(2,1)S(1)} %shard_map.122.refs_0_), channel_id=1, source_target_pairs={{0,24},{2,26},{4,28},{6,30},{8,16},{10,18},{12,20},{14,22},{16,8},... | collective-permute-start | bytes 110600 | tf_op jit(solution)/shard_map/ppermute | solution.py:243
  43.2 1.4 %collective-permute-start.16 = (bf16[8,64,128]{2,1,0:T(8,128)(2,1)S(1)}, bf16[8,64,128]{2,1,0:T(8,128)(2,1)S(1)}, u32[]{:S(2)}, u32[]{:S(2)}) collective-permute-start(bf16[8,64,128]{2,1,0:T(8,128)(2,1)S(1)} %collective-permute-done.9.g2), channel_id=1, source_target_pairs={{0,2},{2,0},{4,6},{6,4},{8,10},{10,8},{12,14},{14,12},{16,18},{18,... | collective-permute-start | bytes 393224 | tf_op jit(solution)/shard_map/ppermute | solution.py:243
where the time goes:
time: 46.8 us; the launch traced here: 46.3 us
  starting transfers between devices  17.2 us (37%)
  waiting for transfers between devices  16.2 us (35%)
  Pallas kernels  11.5 us (25%)
  between operations  1.42 us (3%)
    ppermute x17, starting transfers between devices, moved(): return lax.ppermute(block, axis, [(i, target(i) % n) for i in range(n)])  17.2 us
    ppermute x17, waiting for transfers between devices, moved(): return lax.ppermute(block, axis, [(i, target(i) % n) for i in range(n)])  16.2 us
    pallas_call x1, Pallas kernels, shards(): call(forward_swap_kernel, [tiles, piece, piece, slots, slots], [SMEM] + [...  2.86 us
    pallas_call x2, Pallas kernels, shards(): call(functools.partial(middle_kernel, parts, first), [half_rows, half_col...  1.81 us
    pallas_call x1, Pallas kernels, shards(): call(backward_last_kernel, [jax.ShapeDtypeStruct((width, nodes), BF16), j...  1.74 us
    pallas_call x1, Pallas kernels, shards(): call(forward_send_kernel, [totals, piece], [SMEM] * 3 + [VMEM] * 2, [VMEM...  1.2 us
    pallas_call x1, Pallas kernels, shards(): call(backward_near_kernel, [totals, totals], [SMEM] * 3 + [VMEM] * 3, [VM...  1.04 us
    pallas_call x1, Pallas kernels, shards(): call(forward_own_kernel, [totals], [SMEM] * 3 + [VMEM] * 2, [VMEM], (), f...  1.01 us
  transfers between devices with their start and end apart: 17, of which 9 were waited for; matrix products, arithmetic and copies ran while one was open for 0% of the time, Pallas kernels for 15%

commit v1 on v0

--- a/solution.py
+++ b/solution.py
@@ -173,7 +173,7 @@
 
 
 def weight_grad_kernel(n, *refs):
-    hts, grads, acts, (out, wg, sems) = refs[:n], refs[n : 2 * n], refs[2 * n : 3 * n], refs[3 * n :]
+    hts, grads, acts, (out, mine, other, sems) = refs[:n], refs[n : 2 * n], refs[2 * n : 3 * n], refs[3 * n :]
     copies, first = [], 0
     for i, act in enumerate(acts):
         rows = act.shape[0]
@@ -181,9 +181,26 @@
         copies[-1].start()
         first += rows
     full = sum(jnp.dot(h[...], g[...], preferred_element_type=F32) for h, g in zip(hts, grads))
-    wg[...] = full[: wg.shape[0]].astype(wg.dtype)
+    full = full.astype(BF16)
+    rows = mine.shape[0]
+    low, high = full[:rows], full[rows:]
+    first = own_core() == 0
+    mine[...] = jnp.where(first, low, high)
+    other[...] = jnp.where(first, high, low)
     for c in copies:
         c.wait()
+
+
+def swap_payload_kernel(g, *refs):
+    parts, out = refs[:-1], refs[-1]
+    blocks, width, _ = g.shape
+    for b in range(blocks):
+        out[b * width : (b + 1) * width, :] = g[b]
+    total = paired_sum([r[...] for r in parts]).astype(BF16)
+    rows, hid = total.shape
+    if hid < out.shape[1]:
+        out[blocks * width :, :] = jnp.zeros((rows, out.shape[1]), BF16)
+    out[blocks * width :, :hid] = total
 
 
 def pull(g, tiles, src, dst, acc, j, o, live):
@@ -212,19 +229,29 @@
     slot_loop(count[0], tiles.shape[0], (2, far), body)
 
 
-def backward_last_kernel(count, src, dst, tiles, g, acc0, acc2, accd, *refs):
-    parts, (out, wg, bias, acc) = refs[:-4], refs[-4:]
-    blocks = g.shape[0]
+def backward_last_kernel(count, src, dst, tiles, sent, got, acc0, acc2, accd, out, wg, bias, acc):
+    blocks, width = acc.shape[0] - 1, acc.shape[1]
+    f_in, hid = wg.shape
     acc[...] = jnp.zeros_like(acc)
-    far = 3 - 2 * own_core()
-    slot_loop(count[0], tiles.shape[0], (far,), functools.partial(pull, g, tiles, src, dst, acc))
+    core = own_core()
+    far = 3 - 2 * core
+
+    def body(j, o, live):
+        k = j * REACH + o
+        s = jnp.where(live, src[k], blocks)
+        d = pl.multiple_of((dst[k] - o * blocks) * width, width)
+        acc[s] += jnp.dot(got[pl.ds(d, width), :], tiles[j, o], preferred_element_type=F32)
+
+    slot_loop(count[0], tiles.shape[0], (far,), body)
     for b in range(blocks):
         total = acc[b] + acc0[b] + acc2[b] + accd[b]
         out[:, b * BLOCK : (b + 1) * BLOCK] = total.astype(BF16)
-    whole = paired_sum([r[...] for r in parts])
-    f_in = wg.shape[0]
-    wg[...] = whole[:f_in]
-    bias[...] = whole[f_in : f_in + 1]
+    a, b = (r[blocks * width :, :hid].astype(F32) for r in (sent, got))
+    low, high = jnp.where(core == 0, a, b), jnp.where(core == 0, b, a)
+    rows = low.shape[0]
+    wg[:rows, :] = low
+    wg[rows:, :] = high[: f_in - rows]
+    bias[...] = high[f_in - rows : f_in - rows + 1]
 
 
 def paired_sum(parts):
@@ -270,7 +297,7 @@
     tiles = jax.ShapeDtypeStruct((groups, REACH, BLOCK, BLOCK), BF16)
     slots = jax.ShapeDtypeStruct((capacity,), jnp.int32)
     rows = jax.ShapeDtypeStruct((nodes, hid), BF16)
-    gradient = jax.ShapeDtypeStruct((f_in + 16, hid), BF16)
+    gradient = jax.ShapeDtypeStruct(((f_in + 32) // 2, hid), BF16)
     m = groups_at_once(groups)
     flops = 2 * capacity * BLOCK * BLOCK * width // REACH
 
@@ -300,7 +327,7 @@
     half = jax.ShapeDtypeStruct((blocks // cut, width, BLOCK), BF16)
     half_wide = jax.ShapeDtypeStruct(half.shape, F32)
     half_rows = jax.ShapeDtypeStruct((nodes // cut, hid), BF16)
-    half_columns = jax.ShapeDtypeStruct((f_in + 16, nodes // cut), BF16)
+    half_columns = jax.ShapeDtypeStruct((f_in + 32, nodes // cut), BF16)
     chip = call(functools.partial(sum_kernel, 2, 0), [half] * cut, [VMEM] * 2, [VMEM] * cut)(acc2, swap)
     chip = [moved(c, "dom", lambda i: i + 2) for c in chip]
     direct = moved(direct, "dom", lambda i: i + 1 + 2 * (i % 2))
@@ -323,29 +350,30 @@
         hts.append(ht)
         grads.append(grad)
         g_list += [g_own] + [moved(g, "feat", lambda i, q=q + 1: i + q) for q, g in enumerate(g_others)]
-    output, wg = call(
+    output, wg, wg_other = call(
         functools.partial(weight_grad_kernel, cut),
-        [rows, gradient],
+        [rows, gradient, gradient],
         [VMEM] * (3 * cut),
-        [HBM, VMEM],
+        [HBM, VMEM, VMEM],
         [pltpu.SemaphoreType.DMA((cut,))],
         2 * nodes * f_in * hid,
     )(*hts, *grads, *acts)
     r, *more = radices(lax.axis_size("dom"))
-    wgs = exchanged(wg, "dom", 1, r)
-    g_list[0], wgs[1] = lax.optimization_barrier((g_list[0], wgs[1]))
+    wgs = [wg] + [moved(wg_other if s % 2 else wg, "dom", lambda i, s=s: i ^ s) for s in range(1, r)]
+    g_list[0], *wgs = lax.optimization_barrier((g_list[0], *wgs))
     (g,) = call(functools.partial(join_kernel, parts), [piece], [VMEM] * len(g_list), [VMEM])(*g_list)
     g_chip = moved(g, "dom", lambda i: i - 2)
     g_direct = moved(g, "dom", lambda i: i - 3 + 2 * (i % 2))
     (back0,) = call(backward_own_kernel, [totals], [SMEM] * 3 + [VMEM] * 2, [VMEM], (), flops)(*index, tiles, g)
     stride = r
     for r in more:
-        back0, *wgs = lax.optimization_barrier((back0, *wgs))
         (wg,) = call(paired_sum_kernel, [gradient], [VMEM] * len(wgs), [VMEM])(*wgs)
         wgs = exchanged(wg, "dom", stride, r)
         stride *= r
-    g_chip, g_direct, *wgs = lax.optimization_barrier((g_chip, g_direct, *wgs))
-    g_swap = moved(g_chip, "dom", swapped)
+    back0, g_chip, g_direct, *wgs = lax.optimization_barrier((back0, g_chip, g_direct, *wgs))
+    payload = jax.ShapeDtypeStruct((blocks * width + gradient.shape[0], BLOCK), BF16)
+    (sent,) = call(swap_payload_kernel, [payload], [VMEM] * (1 + len(wgs)), [VMEM])(g_chip, *wgs)
+    got = moved(sent, "dom", swapped)
     back2, backd = call(
         backward_near_kernel, [totals, totals], [SMEM] * 3 + [VMEM] * 3, [VMEM] * 2, (), 2 * flops
     )(*index, tiles, g_chip, g_direct)
@@ -356,11 +384,11 @@
             jax.ShapeDtypeStruct((f_in, hid), F32),
             jax.ShapeDtypeStruct((1, hid), F32),
         ],
-        [SMEM] * 3 + [VMEM] * (5 + len(wgs)),
+        [SMEM] * 3 + [VMEM] * 6,
         [VMEM] * 3,
         [acc],
         flops,
-    )(*index, tiles, g_swap, back0, back2, backd, *wgs)
+    )(*index, tiles, sent, got, back0, back2, backd)
     return output, weight_grad, bias_grad.reshape(hid), input_grad.T
 
 

time: 46.8 us -> 43.3 us (0.925); the launches traced: 46.3 us -> 43.4 us
  waiting for transfers between devices: 16.2 us -> 9.87 us
  starting transfers between devices: 17.2 us -> 20.6 us
    ppermute x17, waiting for transfers between devices: 16.2 us -> 9.87 us  [moved(): return lax.ppermute(block, axis, [(i, target(i) % n) for i in range(n)])]
    ppermute x17, starting transfers between devices: 17.2 us -> 20.6 us  [moved(): return lax.ppermute(block, axis, [(i, target(i) % n) for i in range(n)])]
  transfers between devices with their start and end apart: 17 -> 17, of which waited for: 9 -> 7; matrix products, arithmetic and copies ran while one was open for 0% -> 0% of each run, Pallas kernels for 15% -> 16%
where the time goes in v1:
time: 43.3 us; the launch traced here: 43.4 us
  starting transfers between devices  20.6 us (48%)
  Pallas kernels  11.5 us (27%)
  waiting for transfers between devices  9.87 us (23%)
  between operations  1.42 us (3%)
    ppermute x17, starting transfers between devices, moved(): return lax.ppermute(block, axis, [(i, target(i) % n) for i in range(n)])  20.6 us
    ppermute x17, waiting for transfers between devices, moved(): return lax.ppermute(block, axis, [(i, target(i) % n) for i in range(n)])  9.87 us
    pallas_call x1, Pallas kernels, shards(): call(forward_swap_kernel, [tiles, piece, piece, slots, slots], [SMEM] + [...  2.86 us
    pallas_call x2, Pallas kernels, shards(): call(functools.partial(middle_kernel, parts, first), [half_rows, half_col...  1.81 us
    pallas_call x1, Pallas kernels, shards(): call(backward_last_kernel, [jax.ShapeDtypeStruct((width, nodes), BF16), j...  1.74 us
    pallas_call x1, Pallas kernels, shards(): call(forward_send_kernel, [totals, piece], [SMEM] * 3 + [VMEM] * 2, [VMEM...  1.2 us
    pallas_call x1, Pallas kernels, shards(): call(backward_near_kernel, [totals, totals], [SMEM] * 3 + [VMEM] * 3, [VM...  1.04 us
    pallas_call x1, Pallas kernels, shards(): call(forward_own_kernel, [totals], [SMEM] * 3 + [VMEM] * 2, [VMEM], (), f...  1.02 us
  transfers between devices with their start and end apart: 17, of which 7 were waited for; matrix products, arithmetic and copies ran while one was open for 0% of the time, Pallas kernels for 16%

profile of v1, /device:TPU:0, one launch (start us, length us, event | category | flops | bytes accessed | tf_op | source)
XLA Modules:
  0.0 43.4 jit_solution(3351166258207487168)
XLA Ops:
  1.3 2.9 %shard_map.111 = (bf16[24,4,128,128]{3,2,1,0:T(8,128)(2,1)S(1)}, bf16[8,64,128]{2,1,0:T(8,128)(2,1)S(1)}, bf16[8,64,128]{2,1,0:T(8,128)(2,1)S(1)}, s32[96]{0:T(128)S(1)}, s32[96]{0:T(128)S(1)}) custom-call(s32[1]{0:T(128)S(6)} %copy.12.count, s32[96]{0:T(128)} %src_hbm.1, s32[96]{0:T(128)} %dst_hbm.1, bf16[1024,128]{1,0:T(8,128)(2,1)} %x_hbm.1, ...), custom_call_target="tpu_custom_call" | custom-call | flops 50331648 | bytes 1048576 | tf_op jit(solution)/shard_map/pallas_call | solution.py:307
  4.9 1.2 %shard_map.113 = (f32[9,64,128]{2,1,0:T(8,128)S(1)}, bf16[8,64,128]{2,1,0:T(8,128)(2,1)S(1)}) custom-call(s32[1]{0:T(128)S(6)} %copy.12.count, s32[96]{0:T(128)S(1)} %get-tuple-element.43.src, s32[96]{0:T(128)S(1)} %get-tuple-element.44.dst, bf16[8,64,128]{2,1,0:T(8,128)(2,1)S(1)} %get-tuple-element.45.xt, bf16[24,4,128,128]{3,2,1,0:T(8,128)(2,1)S(1)} %get-tuple-element.46.tiles), custom_call_target="tpu_custom_call" | custom-call | flops 100663296 | bytes 1048576 | tf_op jit(solution)/shard_map/pallas_call | solution.py:322
  6.5 3.1 %collective-permute-start.4 = (bf16[4,64,128]{2,1,0:T(8,128)(2,1)S(1)}, bf16[4,64,128]{2,1,0:T(8,128)(2,1)S(1)}, u32[]{:S(2)}, u32[]{:S(2)}) collective-permute-start(bf16[4,64,128]{2,1,0:T(8,128)(2,1)S(1)} %get-tuple-element.52), channel_id=1, source_target_pairs={{0,4},{2,6},{4,8},{6,10},{8,12},{10,14},{12,16},{14,18},{16,20},{1... | collective-permute-start | bytes 196616 | tf_op jit(solution)/shard_map/ppermute | solution.py:270
  9.6 2.5 %collective-permute-start.2 = (bf16[4,64,128]{2,1,0:T(8,128)(2,1)S(1)}, bf16[4,64,128]{2,1,0:T(8,128)(2,1)S(1)}, u32[]{:S(2)}, u32[]{:S(2)}) collective-permute-start(bf16[4,64,128]{2,1,0:T(8,128)(2,1)S(1)} %get-tuple-element.50), channel_id=1, source_target_pairs={{0,4},{2,6},{4,8},{6,10},{8,12},{10,14},{12,16},{14,18},{16,20},{1... | collective-permute-start | bytes 196616 | tf_op jit(solution)/shard_map/ppermute | solution.py:270
  12.0 1.0 %shard_map.112.refs_0_ = f32[9,64,128]{2,1,0:T(8,128)S(1)} custom-call(s32[1]{0:T(128)S(6)} %copy.12.count, s32[96]{0:T(128)S(1)} %get-tuple-element.43.src, s32[96]{0:T(128)S(1)} %get-tuple-element.44.dst, bf16[8,64,128]{2,1,0:T(8,128)(2,1)S(1)} %get-tuple-element.45.xt, bf16[24,4,128,128]{3,2,1,0:T(8,128)(2,1)S(1)} %get-tuple-element.46.tiles), custom_call_target="tpu_custom_call" | custom-call | flops 50331648 | bytes 1048576 | tf_op jit(solution)/shard_map/pallas_call | solution.py:334
  13.0 0.8 %collective-permute-done.refs_1_ = bf16[8,64,128]{2,1,0:T(8,128)(2,1)S(1)} collective-permute-done((bf16[8,64,128]{2,1,0:T(8,128)(2,1)S(1)}, bf16[8,64,128]{2,1,0:T(8,128)(2,1)S(1)}, u32[]{:S(2)}, u32[]{:S(2)}) %collective-permute-start) | collective-permute-done | bytes 131104 | tf_op jit(solution)/shard_map/ppermute | solution.py:270
  13.8 3.1 %collective-permute-done.4.refs_2_ = bf16[4,64,128]{2,1,0:T(8,128)(2,1)S(1)} collective-permute-done((bf16[4,64,128]{2,1,0:T(8,128)(2,1)S(1)}, bf16[4,64,128]{2,1,0:T(8,128)(2,1)S(1)}, u32[]{:S(2)}, u32[]{:S(2)}) %collective-permute-start.4) | collective-permute-done | bytes 65568 | tf_op jit(solution)/shard_map/ppermute | solution.py:270
  16.9 1.6 %collective-permute-start.5 = (bf16[4,64,128]{2,1,0:T(8,128)(2,1)S(1)}, bf16[4,64,128]{2,1,0:T(8,128)(2,1)S(1)}, u32[]{:S(2)}, u32[]{:S(2)}) collective-permute-start(bf16[4,64,128]{2,1,0:T(8,128)(2,1)S(1)} %shard_map.117.refs_0_), channel_id=1, source_target_pairs={{0,1},{1,0},{2,3},{3,2},{4,5},{5,4},{6,7},{7,6},{8,9},{9,8},{10,11... | collective-permute-start | bytes 196616 | tf_op jit(solution)/shard_map/ppermute | solution.py:270
  18.5 1.4 %collective-permute-start.3 = (bf16[4,64,128]{2,1,0:T(8,128)(2,1)S(1)}, bf16[4,64,128]{2,1,0:T(8,128)(2,1)S(1)}, u32[]{:S(2)}, u32[]{:S(2)}) collective-permute-start(bf16[4,64,128]{2,1,0:T(8,128)(2,1)S(1)} %shard_map.115.refs_0_), channel_id=1, source_target_pairs={{0,1},{1,0},{2,3},{3,2},{4,5},{5,4},{6,7},{7,6},{8,9},{9,8},{10,11... | collective-permute-start | bytes 196616 | tf_op jit(solution)/shard_map/ppermute | solution.py:270
  19.9 1.7 %collective-permute-done.5.refs_1_ = bf16[4,64,128]{2,1,0:T(8,128)(2,1)S(1)} collective-permute-done((bf16[4,64,128]{2,1,0:T(8,128)(2,1)S(1)}, bf16[4,64,128]{2,1,0:T(8,128)(2,1)S(1)}, u32[]{:S(2)}, u32[]{:S(2)}) %collective-permute-start.5) | collective-permute-done | bytes 65568 | tf_op jit(solution)/shard_map/ppermute | solution.py:270
  21.6 0.9 %shard_map.118 = (bf16[512,128]{1,0:T(8,128)(2,1)S(1)}, bf16[160,512]{1,0:T(8,128)(2,1)S(1)}, bf16[512,128]{1,0:T(8,128)(2,1)S(1)}, f32[4,64,128]{2,1,0:T(8,128)S(1)}, bf16[4,64,128]{2,1,0:T(8,128)(2,1)S(1)}) custom-call(f32[1,128]{1,0:T(1,128)S(1)} %bitcast.4, bf16[128,128]{1,0:T(8,128)(2,1)S(1)} %copy-done.1, bf16[1024,128]{1,0:T(8,128)(2,1)S(1)} %copy-done, ...), custom_call_target="tpu_custom_call" | custom-call | flops 33554432 | bytes 1048576 | tf_op jit(solution)/shard_map/pallas_call | solution.py:341
  22.5 1.5 %collective-permute-start.10 = (bf16[4,64,128]{2,1,0:T(8,128)(2,1)S(1)}, bf16[4,64,128]{2,1,0:T(8,128)(2,1)S(1)}, u32[]{:S(2)}, u32[]{:S(2)}) collective-permute-start(bf16[4,64,128]{2,1,0:T(8,128)(2,1)S(1)} %get-tuple-element.65), channel_id=1, source_target_pairs={{0,1},{1,0},{2,3},{3,2},{4,5},{5,4},{6,7},{7,6},{8,9},{9,8},{10,11... | collective-permute-start | bytes 196616 | tf_op jit(solution)/shard_map/ppermute | solution.py:270
  24.0 0.9 %shard_map.116 = (bf16[512,128]{1,0:T(8,128)(2,1)S(1)}, bf16[160,512]{1,0:T(8,128)(2,1)S(1)}, bf16[512,128]{1,0:T(8,128)(2,1)S(1)}, f32[4,64,128]{2,1,0:T(8,128)S(1)}, bf16[4,64,128]{2,1,0:T(8,128)(2,1)S(1)}) custom-call(f32[1,128]{1,0:T(1,128)S(1)} %bitcast.5, bf16[128,128]{1,0:T(8,128)(2,1)S(1)} %copy-done.1, bf16[1024,128]{1,0:T(8,128)(2,1)S(1)} %copy-done, ...), custom_call_target="tpu_custom_call" | custom-call | flops 33554432 | bytes 1048576 | tf_op jit(solution)/shard_map/pallas_call | solution.py:341
  24.9 0.8 %collective-permute-start.9 = (bf16[4,64,128]{2,1,0:T(8,128)(2,1)S(1)}, bf16[4,64,128]{2,1,0:T(8,128)(2,1)S(1)}, u32[]{:S(2)}, u32[]{:S(2)}) collective-permute-start(bf16[4,64,128]{2,1,0:T(8,128)(2,1)S(1)} %get-tuple-element.63), channel_id=1, source_target_pairs={{0,1},{1,0},{2,3},{3,2},{4,5},{5,4},{6,7},{7,6},{8,9},{9,8},{10,11... | collective-permute-start | bytes 196616 | tf_op jit(solution)/shard_map/ppermute | solution.py:270
  25.8 0.7 %shard_map.119 = (bf16[1024,128]{1,0:T(8,128)(2,1)}, bf16[80,128]{1,0:T(8,128)(2,1)S(1)}, bf16[80,128]{1,0:T(8,128)(2,1)S(1)}) custom-call(bf16[160,512]{1,0:T(8,128)(2,1)S(1)} %get-tuple-element.51.refs_0_, bf16[160,512]{1,0:T(8,128)(2,1)S(1)} %get-tuple-element.53.refs_1_, bf16[512,128]{1,0:T(8,128)(2,1)S(1)} %get-tuple-element.54.refs_2_, ...), custom_call_target="tpu_custom_call" | custom-call | flops 33554432 | bytes 1048576 | tf_op jit(solution)/shard_map/pallas_call | solution.py:353
  26.7 1.8 %collective-permute-start.8 = (bf16[80,128]{1,0:T(8,128)(2,1)S(1)}, bf16[80,128]{1,0:T(8,128)(2,1)S(1)}, u32[]{:S(2)}, u32[]{:S(2)}) collective-permute-start(bf16[80,128]{1,0:T(8,128)(2,1)S(1)} %get-tuple-element.61), channel_id=1, source_target_pairs={{0,6},{2,4},{4,2},{6,0},{8,14},{10,12},{12,10},{14,8},{16,22},{18,... | collective-permute-start | bytes 61448 | tf_op jit(solution)/shard_map/ppermute | solution.py:270
  28.4 2.0 %collective-permute-done.7.refs_2_ = bf16[80,128]{1,0:T(8,128)(2,1)S(1)} collective-permute-done((bf16[80,128]{1,0:T(8,128)(2,1)S(1)}, bf16[80,128]{1,0:T(8,128)(2,1)S(1)}, u32[]{:S(2)}, u32[]{:S(2)}) %collective-permute-start.7) | collective-permute-done | bytes 20512 | tf_op jit(solution)/shard_map/ppermute | solution.py:270
  30.5 2.2 %collective-permute-start.11 = (bf16[8,64,128]{2,1,0:T(8,128)(2,1)S(1)}, bf16[8,64,128]{2,1,0:T(8,128)(2,1)S(1)}, u32[]{:S(2)}, u32[]{:S(2)}) collective-permute-start(bf16[8,64,128]{2,1,0:T(8,128)(2,1)S(1)} %shard_map.120.g0), channel_id=1, source_target_pairs={{0,28},{2,30},{4,0},{6,2},{8,4},{10,6},{12,8},{14,10},{16,12},{18,... | collective-permute-start | bytes 393224 | tf_op jit(solution)/shard_map/ppermute | solution.py:270
  32.7 1.6 %collective-permute-start.13 = (bf16[80,128]{1,0:T(8,128)(2,1)S(1)}, bf16[80,128]{1,0:T(8,128)(2,1)S(1)}, u32[]{:S(2)}, u32[]{:S(2)}) collective-permute-start(bf16[80,128]{1,0:T(8,128)(2,1)S(1)} %shard_map.122.refs_0_), channel_id=1, source_target_pairs={{0,8},{2,10},{4,12},{6,14},{8,0},{10,2},{12,4},{14,6},{16,24},{18,... | collective-permute-start | bytes 61448 | tf_op jit(solution)/shard_map/ppermute | solution.py:270
  34.6 2.6 %collective-permute-start.15 = (bf16[80,128]{1,0:T(8,128)(2,1)S(1)}, bf16[80,128]{1,0:T(8,128)(2,1)S(1)}, u32[]{:S(2)}, u32[]{:S(2)}) collective-permute-start(bf16[80,128]{1,0:T(8,128)(2,1)S(1)} %shard_map.122.refs_0_), channel_id=1, source_target_pairs={{0,24},{2,26},{4,28},{6,30},{8,16},{10,18},{12,20},{14,22},{16,8},... | collective-permute-start | bytes 61448 | tf_op jit(solution)/shard_map/ppermute | solution.py:270
  37.2 1.0 %shard_map.121.acc0 = f32[9,64,128]{2,1,0:T(8,128)S(1)} custom-call(s32[1]{0:T(128)S(6)} %copy.12.count, s32[96]{0:T(128)S(1)} %get-tuple-element.43.src, s32[96]{0:T(128)S(1)} %get-tuple-element.44.dst, bf16[24,4,128,128]{3,2,1,0:T(8,128)(2,1)S(1)} %get-tuple-element.46.tiles, bf16[8,64,128]{2,1,0:T(8,128)(2,1)S(1)} %shard_map.120.g0), custom_call_target="tpu_custom_call" | custom-call | flops 50331648 | bytes 1048576 | tf_op jit(solution)/shard_map/pallas_call | solution.py:367
  38.2 1.3 %collective-permute-done.13.refs_1_ = bf16[80,128]{1,0:T(8,128)(2,1)S(1)} collective-permute-done((bf16[80,128]{1,0:T(8,128)(2,1)S(1)}, bf16[80,128]{1,0:T(8,128)(2,1)S(1)}, u32[]{:S(2)}, u32[]{:S(2)}) %collective-permute-start.13) | collective-permute-done | bytes 20512 | tf_op jit(solution)/shard_map/ppermute | solution.py:270
  40.3 1.0 %shard_map.124 = (f32[9,64,128]{2,1,0:T(8,128)S(1)}, f32[9,64,128]{2,1,0:T(8,128)S(1)}) custom-call(s32[1]{0:T(128)S(6)} %copy.12.count, s32[96]{0:T(128)S(1)} %get-tuple-element.43.src, s32[96]{0:T(128)S(1)} %get-tuple-element.44.dst, bf16[24,4,128,128]{3,2,1,0:T(8,128)(2,1)S(1)} %get-tuple-element.46.tiles, ...), custom_call_target="tpu_custom_call" | custom-call | flops 100663296 | bytes 1048576 | tf_op jit(solution)/shard_map/pallas_call | solution.py:377
  41.6 1.7 %shard_map.125 = (bf16[64,1024]{1,0:T(8,128)(2,1)}, f32[128,128]{1,0:T(8,128)}, f32[1,128]{1,0:T(1,128)}) custom-call(s32[1]{0:T(128)S(6)} %copy.12.count, s32[96]{0:T(128)S(1)} %get-tuple-element.43.src, s32[96]{0:T(128)S(1)} %get-tuple-element.44.dst, bf16[24,4,128,128]{3,2,1,0:T(8,128)(2,1)S(1)} %get-tuple-element.46.tiles, ...), custom_call_target="tpu_custom_call" | custom-call | flops 50331648 | bytes 1048576 | tf_op jit(solution)/shard_map/pallas_call | solution.py:380
  (31 shorter events, 2.7 us)
Async XLA Ops:
  4.1 2.3 %collective-permute-start.1 = (bf16[8,64,128]{2,1,0:T(8,128)(2,1)S(1)}, bf16[8,64,128]{2,1,0:T(8,128)(2,1)S(1)}, u32[]{:S(2)}, u32[]{:S(2)}) collective-permute-start(bf16[8,64,128]{2,1,0:T(8,128)(2,1)S(1)} %get-tuple-element.49), channel_id=1, source_target_pairs={{0,2},{2,0},{4,6},{6,4},{8,10},{10,8},{12,14},{14,12},{16,18},{18,... | collective-permute-start | bytes 393224 | tf_op jit(solution)/shard_map/ppermute | solution.py:270
  6.1 15.5 %copy-start = (bf16[1024,128]{1,0:T(8,128)(2,1)S(1)}, bf16[1024,128]{1,0:T(8,128)(2,1)}, u32[]{:S(2)}) copy-start(bf16[1024,128]{1,0:T(8,128)(2,1)} %og_ref.3) | copy-start | bytes 786436
  6.1 15.5 %copy-start.1 = (bf16[128,128]{1,0:T(8,128)(2,1)S(1)}, bf16[128,128]{1,0:T(8,128)(2,1)}, u32[]{:S(2)}) copy-start(bf16[128,128]{1,0:T(8,128)(2,1)} %w_ref.3) | copy-start | bytes 98308
  6.1 15.5 %copy-start.2 = (f32[128]{0:T(128)S(1)}, f32[128]{0:T(128)}, u32[]{:S(2)}) copy-start(f32[128]{0:T(128)} %param.10) | copy-start | bytes 1540
  6.1 7.7 %collective-permute-start = (bf16[8,64,128]{2,1,0:T(8,128)(2,1)S(1)}, bf16[8,64,128]{2,1,0:T(8,128)(2,1)S(1)}, u32[]{:S(2)}, u32[]{:S(2)}) collective-permute-start(bf16[8,64,128]{2,1,0:T(8,128)(2,1)S(1)} %get-tuple-element.47), channel_id=1, source_target_pairs={{0,2},{2,8},{4,6},{6,12},{8,10},{10,16},{12,14},{14,20},{16,18},{1... | collective-permute-start | bytes 393224 | tf_op jit(solution)/shard_map/ppermute | solution.py:270
  6.5 10.4 %collective-permute-start.4 = (bf16[4,64,128]{2,1,0:T(8,128)(2,1)S(1)}, bf16[4,64,128]{2,1,0:T(8,128)(2,1)S(1)}, u32[]{:S(2)}, u32[]{:S(2)}) collective-permute-start(bf16[4,64,128]{2,1,0:T(8,128)(2,1)S(1)} %get-tuple-element.52), channel_id=1, source_target_pairs={{0,4},{2,6},{4,8},{6,10},{8,12},{10,14},{12,16},{14,18},{16,20},{1... | collective-permute-start | bytes 196616 | tf_op jit(solution)/shard_map/ppermute | solution.py:270
  9.6 8.9 %collective-permute-start.2 = (bf16[4,64,128]{2,1,0:T(8,128)(2,1)S(1)}, bf16[4,64,128]{2,1,0:T(8,128)(2,1)S(1)}, u32[]{:S(2)}, u32[]{:S(2)}) collective-permute-start(bf16[4,64,128]{2,1,0:T(8,128)(2,1)S(1)} %get-tuple-element.50), channel_id=1, source_target_pairs={{0,4},{2,6},{4,8},{6,10},{8,12},{10,14},{12,16},{14,18},{16,20},{1... | collective-permute-start | bytes 196616 | tf_op jit(solution)/shard_map/ppermute | solution.py:270
  16.9 4.7 %collective-permute-start.5 = (bf16[4,64,128]{2,1,0:T(8,128)(2,1)S(1)}, bf16[4,64,128]{2,1,0:T(8,128)(2,1)S(1)}, u32[]{:S(2)}, u32[]{:S(2)}) collective-permute-start(bf16[4,64,128]{2,1,0:T(8,128)(2,1)S(1)} %shard_map.117.refs_0_), channel_id=1, source_target_pairs={{0,1},{1,0},{2,3},{3,2},{4,5},{5,4},{6,7},{7,6},{8,9},{9,8},{10,11... | collective-permute-start | bytes 196616 | tf_op jit(solution)/shard_map/ppermute | solution.py:270
  18.5 5.5 %collective-permute-start.3 = (bf16[4,64,128]{2,1,0:T(8,128)(2,1)S(1)}, bf16[4,64,128]{2,1,0:T(8,128)(2,1)S(1)}, u32[]{:S(2)}, u32[]{:S(2)}) collective-permute-start(bf16[4,64,128]{2,1,0:T(8,128)(2,1)S(1)} %shard_map.115.refs_0_), channel_id=1, source_target_pairs={{0,1},{1,0},{2,3},{3,2},{4,5},{5,4},{6,7},{7,6},{8,9},{9,8},{10,11... | collective-permute-start | bytes 196616 | tf_op jit(solution)/shard_map/ppermute | solution.py:270
  22.5 7.9 %collective-permute-start.10 = (bf16[4,64,128]{2,1,0:T(8,128)(2,1)S(1)}, bf16[4,64,128]{2,1,0:T(8,128)(2,1)S(1)}, u32[]{:S(2)}, u32[]{:S(2)}) collective-permute-start(bf16[4,64,128]{2,1,0:T(8,128)(2,1)S(1)} %get-tuple-element.65), channel_id=1, source_target_pairs={{0,1},{1,0},{2,3},{3,2},{4,5},{5,4},{6,7},{7,6},{8,9},{9,8},{10,11... | collective-permute-start | bytes 196616 | tf_op jit(solution)/shard_map/ppermute | solution.py:270
  24.9 5.5 %collective-permute-start.9 = (bf16[4,64,128]{2,1,0:T(8,128)(2,1)S(1)}, bf16[4,64,128]{2,1,0:T(8,128)(2,1)S(1)}, u32[]{:S(2)}, u32[]{:S(2)}) collective-permute-start(bf16[4,64,128]{2,1,0:T(8,128)(2,1)S(1)} %get-tuple-element.63), channel_id=1, source_target_pairs={{0,1},{1,0},{2,3},{3,2},{4,5},{5,4},{6,7},{7,6},{8,9},{9,8},{10,11... | collective-permute-start | bytes 196616 | tf_op jit(solution)/shard_map/ppermute | solution.py:270
  26.5 1.9 %collective-permute-start.6 = (bf16[80,128]{1,0:T(8,128)(2,1)S(1)}, bf16[80,128]{1,0:T(8,128)(2,1)S(1)}, u32[]{:S(2)}, u32[]{:S(2)}) collective-permute-start(bf16[80,128]{1,0:T(8,128)(2,1)S(1)} %get-tuple-element.61), channel_id=1, source_target_pairs={{0,2},{2,0},{4,6},{6,4},{8,10},{10,8},{12,14},{14,12},{16,18},{18,... | collective-permute-start | bytes 61448 | tf_op jit(solution)/shard_map/ppermute | solution.py:270
  26.6 3.8 %collective-permute-start.7 = (bf16[80,128]{1,0:T(8,128)(2,1)S(1)}, bf16[80,128]{1,0:T(8,128)(2,1)S(1)}, u32[]{:S(2)}, u32[]{:S(2)}) collective-permute-start(bf16[80,128]{1,0:T(8,128)(2,1)S(1)} %get-tuple-element.66.refs_0_), channel_id=1, source_target_pairs={{0,4},{2,6},{4,0},{6,2},{8,12},{10,14},{12,8},{14,10},{16,20},{18,... | collective-permute-start | bytes 61448 | tf_op jit(solution)/shard_map/ppermute | solution.py:270
  26.7 3.8 %collective-permute-start.8 = (bf16[80,128]{1,0:T(8,128)(2,1)S(1)}, bf16[80,128]{1,0:T(8,128)(2,1)S(1)}, u32[]{:S(2)}, u32[]{:S(2)}) collective-permute-start(bf16[80,128]{1,0:T(8,128)(2,1)S(1)} %get-tuple-element.61), channel_id=1, source_target_pairs={{0,6},{2,4},{4,2},{6,0},{8,14},{10,12},{12,10},{14,8},{16,22},{18,... | collective-permute-start | bytes 61448 | tf_op jit(solution)/shard_map/ppermute | solution.py:270
  30.5 9.7 %collective-permute-start.11 = (bf16[8,64,128]{2,1,0:T(8,128)(2,1)S(1)}, bf16[8,64,128]{2,1,0:T(8,128)(2,1)S(1)}, u32[]{:S(2)}, u32[]{:S(2)}) collective-permute-start(bf16[8,64,128]{2,1,0:T(8,128)(2,1)S(1)} %shard_map.120.g0), channel_id=1, source_target_pairs={{0,28},{2,30},{4,0},{6,2},{8,4},{10,6},{12,8},{14,10},{16,12},{18,... | collective-permute-start | bytes 393224 | tf_op jit(solution)/shard_map/ppermute | solution.py:270
  32.7 7.4 %collective-permute-start.12 = (bf16[8,64,128]{2,1,0:T(8,128)(2,1)S(1)}, bf16[8,64,128]{2,1,0:T(8,128)(2,1)S(1)}, u32[]{:S(2)}, u32[]{:S(2)}) collective-permute-start(bf16[8,64,128]{2,1,0:T(8,128)(2,1)S(1)} %shard_map.120.g0), channel_id=1, source_target_pairs={{0,26},{2,0},{4,30},{6,4},{8,2},{10,8},{12,6},{14,12},{16,10},{18,... | collective-permute-start | bytes 393224 | tf_op jit(solution)/shard_map/ppermute | solution.py:270
  32.7 6.7 %collective-permute-start.13 = (bf16[80,128]{1,0:T(8,128)(2,1)S(1)}, bf16[80,128]{1,0:T(8,128)(2,1)S(1)}, u32[]{:S(2)}, u32[]{:S(2)}) collective-permute-start(bf16[80,128]{1,0:T(8,128)(2,1)S(1)} %shard_map.122.refs_0_), channel_id=1, source_target_pairs={{0,8},{2,10},{4,12},{6,14},{8,0},{10,2},{12,4},{14,6},{16,24},{18,... | collective-permute-start | bytes 61448 | tf_op jit(solution)/shard_map/ppermute | solution.py:270
  34.3 5.2 %collective-permute-start.14 = (bf16[80,128]{1,0:T(8,128)(2,1)S(1)}, bf16[80,128]{1,0:T(8,128)(2,1)S(1)}, u32[]{:S(2)}, u32[]{:S(2)}) collective-permute-start(bf16[80,128]{1,0:T(8,128)(2,1)S(1)} %shard_map.122.refs_0_), channel_id=1, source_target_pairs={{0,16},{2,18},{4,20},{6,22},{8,24},{10,26},{12,28},{14,30},{16,0},... | collective-permute-start | bytes 61448 | tf_op jit(solution)/shard_map/ppermute | solution.py:270
  34.6 5.6 %collective-permute-start.15 = (bf16[80,128]{1,0:T(8,128)(2,1)S(1)}, bf16[80,128]{1,0:T(8,128)(2,1)S(1)}, u32[]{:S(2)}, u32[]{:S(2)}) collective-permute-start(bf16[80,128]{1,0:T(8,128)(2,1)S(1)} %shard_map.122.refs_0_), channel_id=1, source_target_pairs={{0,24},{2,26},{4,28},{6,30},{8,16},{10,18},{12,20},{14,22},{16,8},... | collective-permute-start | bytes 61448 | tf_op jit(solution)/shard_map/ppermute | solution.py:270
  40.2 1.4 %collective-permute-start.16 = (bf16[592,128]{1,0:T(8,128)(2,1)S(1)}, bf16[592,128]{1,0:T(8,128)(2,1)S(1)}, u32[]{:S(2)}, u32[]{:S(2)}) collective-permute-start(bf16[592,128]{1,0:T(8,128)(2,1)S(1)} %shard_map.123.sent), channel_id=1, source_target_pairs={{0,2},{2,0},{4,6},{6,4},{8,10},{10,8},{12,14},{14,12},{16,18},{18,... | collective-permute-start | bytes 454664 | tf_op jit(solution)/shard_map/ppermute | solution.py:270
